TPU v7x, 32 devices: a whole 2x2x4 slice. The times are simulated.
32 devices in a mesh: shard: 8 (over z, y), blk: 4 (over x, core).
Axes of the slice: x: 2, y: 2, z: 4, core: 2. Of those that a mesh axis runs over, the one named last changes fastest.
Arguments:
- request_embeddings: bfloat16 [8192, 256], P(('shard', 'blk')), may hold values from -0.5 to 0.5
- frequent_entry_matrix: bfloat16 [2048, 256], replicated, may hold values from -0.23925781 to 0.23925781
- rare_entry_matrix: float32 [16384, 256], P('shard'), may hold values from -0.24 to 0.24
- frequent_entry_lines: int32 [8192, 4], P(('shard', 'blk')), may hold values from 0 to 2047
- rare_place_parent: int32 [8192, 4], P(('shard', 'blk')), may hold values from 0 to 7, all different within a row; in each aligned block of 256 rows (0 to 255, 256 to 511, ...) at most 256 rows name the same one
- rare_local_position: int32 [8192, 4], P(('shard', 'blk')), may hold values from 0 to 2047
- rare_place_tally: int32 [8192], P(('shard', 'blk')), may hold values from 1 to 4
- sharpness_factor: float32 [1], replicated, may hold values from 4 to 16
- pairscore_additive: float32 [1], replicated, may hold values from -6 to -2
Outputs:
- request_derivative: float32 [8192, 256], P(('shard', 'blk'))
- hot_grad: float32 [2048, 256], replicated
- cold_grad: float32 [16384, 256], P(('shard', 'blk'))
Inputs may be any that keep to these rules, and one draw needn't show every extreme that they name: `rare_place_parent`: each row names 4 different owners; among the rows of one device no owner is named by more than 256 rows, a bound that some block reaches.
All inputs are finite; a program needn't handle non-finite values.
Results may differ from a plain program's by a relative error of at most 0.007.
Values may be sent and summed in bfloat16 or wider, within the bound.
A program may use at most 64 MiB of HBM per device.

v0:
```python
import jax
import jax.numpy as jnp
from jax import lax
from jax.sharding import PartitionSpec as P

epsilon = 1e-06


def normalize_rows(vectors):
    radius = jnp.sqrt(jnp.sum(vectors * vectors, axis=1, keepdims=True) + epsilon)
    return (vectors / radius, radius)


def projection_backward(unit_vectors, radius, gradient):
    inner = jnp.sum(unit_vectors * gradient, axis=1, keepdims=True)
    return (gradient - unit_vectors * inner) / radius


def body(
    request_embeddings,
    frequent_entry_matrix,
    rare_entry_matrix,
    frequent_entry_lines,
    rare_place_parent,
    rare_local_position,
    rare_place_tally,
    sharpness_factor,
    pairscore_additive,
):
    pair_count, row_width = request_embeddings.shape
    owner_total = lax.axis_size("shard")
    block_total = lax.axis_size("blk")
    slots_cold = rare_place_parent.shape[1]
    capacity = 2 * pair_count * slots_cold // owner_total
    sharpness_multiplier = sharpness_factor[0]
    additive_term = pairscore_additive[0]
    live_slot = jnp.arange(slots_cold)[None, :] < rare_place_tally[:, None]
    live_flat = live_slot.reshape(-1)
    owner_flat = rare_place_parent.reshape(-1)
    owner_onehot = (
        (owner_flat[:, None] == jnp.arange(owner_total)[None, :]) & live_flat[:, None]
    ).astype(jnp.int32)
    rank_before = jnp.cumsum(owner_onehot, axis=0) - owner_onehot
    position = jnp.sum(rank_before * owner_onehot, axis=1)
    dump_slot = owner_total * capacity
    bucket = jnp.where(live_flat, owner_flat * capacity + position, dump_slot)
    requests = (
        jnp.zeros((dump_slot + 1,), jnp.int32).at[bucket].set(rare_local_position.reshape(-1))
    )
    requests = requests[:dump_slot].reshape(owner_total, capacity)
    received = lax.all_to_all(requests, "shard", split_axis=0, concat_axis=0, tiled=True)
    looked = jnp.take(rare_entry_matrix, received, axis=0)
    fetched = lax.all_to_all(looked, "shard", split_axis=0, concat_axis=0, tiled=True)
    fetched_flat = fetched.reshape(dump_slot, row_width)
    picked = jnp.take(fetched_flat, jnp.minimum(bucket, dump_slot - 1), axis=0) * live_flat[
        :, None
    ].astype(jnp.float32)
    cold_sum = jnp.sum(picked.reshape(pair_count, slots_cold, row_width), axis=1)
    hot_index = jnp.arange(frequent_entry_matrix.shape[0])
    hot_counts = jnp.sum(
        (frequent_entry_lines[:, :, None] == hot_index[None, None, :]).astype(jnp.bfloat16), axis=1
    )
    hot_sum = jnp.dot(hot_counts, frequent_entry_matrix, preferred_element_type=jnp.float32)
    candidate_normalized, candidate_norm = normalize_rows(hot_sum + cold_sum)
    request_normalized, request_norm = normalize_rows(request_embeddings.astype(jnp.float32))
    candidate_reduced = candidate_normalized.astype(jnp.bfloat16)
    request_reduced = request_normalized.astype(jnp.bfloat16)
    my_base = lax.axis_index("blk") * pair_count
    target = my_base + jnp.arange(pair_count)

    def logit_grads(block_rows, first_row):
        pairwise_scores = (
            sharpness_multiplier
            * lax.dot_general(
                request_reduced,
                block_rows,
                (((1,), (1,)), ((), ())),
                preferred_element_type=jnp.float32,
            )
            + additive_term
        )
        column = first_row + jnp.arange(block_rows.shape[0])
        positive = (target[:, None] == column[None, :]).astype(jnp.float32)
        return (jax.nn.sigmoid(pairwise_scores) - positive).astype(jnp.bfloat16)

    group_items, group_queries = (
        lax.all_gather(candidate_reduced, "blk", axis=0, tiled=True),
        lax.all_gather(request_reduced, "blk", axis=0, tiled=True),
    )

    def query_block(block_index, request_running_total):
        first_row = block_index * pair_count
        block_rows = lax.dynamic_slice_in_dim(group_items, first_row, pair_count, 0)
        pairscore_derivative = logit_grads(block_rows, first_row)
        return request_running_total + jnp.dot(
            pairscore_derivative, block_rows, preferred_element_type=jnp.float32
        )

    query_sum = lax.fori_loop(
        0, block_total, query_block, jnp.zeros((pair_count, row_width), jnp.float32)
    )

    def item_block(block_index, item_acc):
        first_row = block_index * pair_count
        query_rows = lax.dynamic_slice_in_dim(group_queries, first_row, pair_count, 0)
        pairwise_scores = (
            sharpness_multiplier
            * lax.dot_general(
                query_rows,
                candidate_reduced,
                (((1,), (1,)), ((), ())),
                preferred_element_type=jnp.float32,
            )
            + additive_term
        )
        row_ids = first_row + jnp.arange(pair_count)
        positive = (row_ids[:, None] == target[None, :]).astype(jnp.float32)
        pairscore_derivative = (jax.nn.sigmoid(pairwise_scores) - positive).astype(jnp.bfloat16)
        return item_acc + lax.dot_general(
            pairscore_derivative,
            query_rows,
            (((0,), (0,)), ((), ())),
            preferred_element_type=jnp.float32,
        )

    candidate_portion = lax.fori_loop(
        0, block_total, item_block, jnp.zeros((pair_count, row_width), jnp.float32)
    )
    request_derivative = projection_backward(
        request_normalized, request_norm, sharpness_multiplier * query_sum
    )
    candidate_derivative = projection_backward(
        candidate_normalized, candidate_norm, sharpness_multiplier * candidate_portion
    ).astype(jnp.bfloat16)
    hot_local = lax.dot_general(
        hot_counts,
        candidate_derivative,
        (((0,), (0,)), ((), ())),
        preferred_element_type=jnp.float32,
    )
    slot_grads = jnp.repeat(candidate_derivative, slots_cold, axis=0)
    outgoing = jnp.zeros((dump_slot + 1, row_width), jnp.bfloat16).at[bucket].set(slot_grads)
    outgoing = outgoing[:dump_slot].reshape(owner_total, capacity, row_width)
    incoming = lax.all_to_all(outgoing, "shard", split_axis=0, concat_axis=0, tiled=True)
    cold_local = (
        jnp.zeros((rare_entry_matrix.shape[0], row_width), jnp.float32)
        .at[received.reshape(-1)]
        .add(incoming.reshape(dump_slot, row_width).astype(jnp.float32))
    )
    hot_grad = lax.psum(hot_local, ("shard", "blk"))
    cold_grad = lax.psum_scatter(cold_local, "blk", scatter_dimension=0, tiled=True)
    return (request_derivative, hot_grad, cold_grad)


def solution(mesh):
    in_specs = (
        P(("shard", "blk"), None),
        P(),
        P("shard", None),
        P(("shard", "blk"), None),
        P(("shard", "blk"), None),
        P(("shard", "blk"), None),
        P(("shard", "blk")),
        P(),
        P(),
    )
    out_specs = (P(("shard", "blk"), None), P(), P(("shard", "blk"), None))
    return jax.shard_map(body, mesh=mesh, in_specs=in_specs, out_specs=out_specs, check_vma=False)
```

profile of v0, /device:TPU:1, one launch (start us, length us, event | category | flops | bytes accessed | tf_op | source)
XLA Modules:
  0.0 312.2 jit_solution(665936090710462185)
XLA Ops:
  8.0 1.0 copy.88
  9.0 0.1 eq.112
  9.2 0.8 lt.151
  10.0 0.7 iota_compare_fusion.3
  10.7 0.2 copy.89
  10.8 0.1 lt.148
  11.0 0.1 lt.157
  11.1 0.7 broadcast_multiply_fusion
  12.1 2.3 reduce-window.6
  14.4 0.3 slice_reduce_fusion
  14.7 0.2 reduce-window.9
  14.9 0.1 copy.96
  15.1 0.1 mul.123
  15.2 0.8 copy.97
  16.0 0.1 reshape.297
  16.2 4.3 %scatter_custom_fusion = s32[2049]{0:T(1024)S(1)} fusion(s32[1024]{0:T(1024)S(1)} %bitcast.74, s32[1024]{0:T(1024)S(1)} %reshape.297, s32[]{:T(128)} %constant.115.clone.1), kind=kCustom, calls=%fused_computation.89 | custom fusion | bytes 8200 | tf_op jit(solution)/shard_map/scatter | solution.py:48
  20.6 11.5 %all_to_all.25 = s32[8,1,256]{2,1,0:T(1,128)S(1)} all-to-all(s32[8,1,256]{2,1,0:T(1,128)S(1)} %bitcast.69), channel_id=1, replica_groups=mesh['shard'=8,'blk'=4] {'shard'}, dimensions={0} | all-to-all | bytes 16384 | tf_op jit(solution)/shard_map/all_to_all | solution.py:51
  32.1 8.6 %gather_fusion = f32[2048,256]{1,0:T(8,128)} fusion(f32[2048,256]{1,0:T(8,128)S(1)} %copy-done, s32[2048]{0:T(1024)S(1)} %broadcast_clamp_fusion), kind=kCustom, calls=%fused_computation | custom fusion | bytes 4202496 | tf_op jit(solution)/shard_map/jit(_take)/gather | solution.py:52
  40.8 3.3 %broadcast_select_fusion = f32[8,256,256]{2,1,0:T(8,128)} fusion(f32[8,256,256]{2,1,0:T(8,128)} %bitcast.64, pred[8,256]{1,0:T(8,128)(4,1)S(1)} %compare_and_fusion), kind=kLoop, calls=%fused_computation.58 | loop fusion | flops 524288 | bytes 4196352 | tf_op jit(solution)/shard_map/jit(_take)/select_n | solution.py:52
  44.0 4.5 %all-to-all-start.1 = ((f32[8,256,256]{2,1,0:T(8,128)}), f32[8,256,256]{2,1,0:T(8,128)}, u32[]{:S(2)}, u32[]{:S(2)}) async-start(f32[8,256,256]{2,1,0:T(8,128)} %broadcast_select_fusion), calls=%async_computation.1 | async-start | bytes 4194304 | tf_op jit(solution)/shard_map/all_to_all | solution.py:53
  48.5 0.1 reduce_sum.72
  48.8 0.8 copy.98
  49.6 0.8 copy.94
  51.2 0.5 copy-done.7
  51.7 0.6 copy-done.2
  52.4 9.6 %all_gather.7 = bf16[1024,256]{0,1:T(8,128)(2,1)} all-gather(bf16[256,256]{0,1:T(8,128)(2,1)S(1)} %fusion.51), channel_id=1, replica_groups=mesh['shard'=8,'blk'=4] {'blk'}, dimensions={0}, use_global_device_ids=true | all-gather | bytes 655360 | tf_op jit(solution)/shard_map/all_gather | solution.py:88
  61.9 1.2 fusion.44
  63.2 31.5 %all-to-all-done.1 = f32[8,256,256]{2,1,0:T(8,128)} async-done(((f32[8,256,256]{2,1,0:T(8,128)}), f32[8,256,256]{2,1,0:T(8,128)}, u32[]{:S(2)}, u32[]{:S(2)}) %all-to-all-start.1) | async-done | bytes 2097184 | tf_op jit(solution)/shard_map/all_to_all | solution.py:53
  94.7 6.3 %gather_fusion.1 = f32[1024,256]{1,0:T(8,128)} fusion(f32[2048,256]{1,0:T(8,128)} %bitcast.9, s32[1024]{0:T(1024)S(1)} %broadcast_clamp_fusion.1), kind=kCustom, calls=%fused_computation.1 | custom fusion | bytes 2101248 | tf_op jit(solution)/shard_map/jit(_take)/gather | solution.py:55
  101.0 2.5 gather.12
  103.5 2.6 multiply_reduce_fusion
  106.1 0.8 copy.99
  106.9 1.8 multiply_reduce_fusion.3
  108.8 0.6 copy-done.9
  109.3 0.7 fusion.61
  110.0 1.7 copy.105
  111.7 14.5 %while.29 = (s32[]{:T(128)}, f32[256,256]{1,0:T(8,128)}, f32[]{:T(128)}, bf16[1024,256]{0,1:T(8,128)(2,1)}, bf16[256,256]{1,0:T(8,128)(2,1)}, /*index=5*/f32[]{:...) while((s32[]{:T(128)}, f32[256,256]{1,0:T(8,128)}, f32[]{:T(128)}, ...), condition=%wide.region_12.13_spmd.clone, body=%wide.region_11.12_spmd.clone.sunk | while | flops 67830280 | bytes 924332 | solution.py:126
  111.7 3.5 %convolution_add_fusion.6 = f32[256,256]{1,0:T(8,128)} fusion(bf16[256,256]{1,0:T(8,128)(2,1)} %get-tuple-element.600, f32[256,256]{1,0:T(8,128)} %get-tuple-element.586, s32[256]{0:T(256)S(1)} %get-tuple-element.539, f32[]{:T(128)} %get-tuple-element.601, bf16[1024,256]{0,1:T(8,128)(2,1)} %get-tuple-element.599, s32[]{:T(128)S(6)} %select_n.132, ...), kind=kOutput, calls=%fused_computation.29.clone.1 | convolution fusion | flops 67829760 | bytes 922112 | tf_op jit(solution)/shard_map/while/body/eval_jaxpr/dot_general | solution.py:119
  115.2 3.6 %convolution_add_fusion.6 = f32[256,256]{1,0:T(8,128)} fusion(bf16[256,256]{1,0:T(8,128)(2,1)} %get-tuple-element.600, f32[256,256]{1,0:T(8,128)} %get-tuple-element.586, s32[256]{0:T(256)S(1)} %get-tuple-element.539, f32[]{:T(128)} %get-tuple-element.601, bf16[1024,256]{0,1:T(8,128)(2,1)} %get-tuple-element.599, s32[]{:T(128)S(6)} %select_n.132, ...), kind=kOutput, calls=%fused_computation.29.clone.1 | convolution fusion | flops 67829760 | bytes 922112 | tf_op jit(solution)/shard_map/while/body/eval_jaxpr/dot_general | solution.py:119
  118.8 3.6 %convolution_add_fusion.6 = f32[256,256]{1,0:T(8,128)} fusion(bf16[256,256]{1,0:T(8,128)(2,1)} %get-tuple-element.600, f32[256,256]{1,0:T(8,128)} %get-tuple-element.586, s32[256]{0:T(256)S(1)} %get-tuple-element.539, f32[]{:T(128)} %get-tuple-element.601, bf16[1024,256]{0,1:T(8,128)(2,1)} %get-tuple-element.599, s32[]{:T(128)S(6)} %select_n.132, ...), kind=kOutput, calls=%fused_computation.29.clone.1 | convolution fusion | flops 67829760 | bytes 922112 | tf_op jit(solution)/shard_map/while/body/eval_jaxpr/dot_general | solution.py:119
  122.5 3.6 %convolution_add_fusion.6 = f32[256,256]{1,0:T(8,128)} fusion(bf16[256,256]{1,0:T(8,128)(2,1)} %get-tuple-element.600, f32[256,256]{1,0:T(8,128)} %get-tuple-element.586, s32[256]{0:T(256)S(1)} %get-tuple-element.539, f32[]{:T(128)} %get-tuple-element.601, bf16[1024,256]{0,1:T(8,128)(2,1)} %get-tuple-element.599, s32[]{:T(128)S(6)} %select_n.132, ...), kind=kOutput, calls=%fused_computation.29.clone.1 | convolution fusion | flops 67829760 | bytes 922112 | tf_op jit(solution)/shard_map/while/body/eval_jaxpr/dot_general | solution.py:119
  126.1 1.8 copy.106
  127.9 1.0 multiply_reduce_fusion.1
  128.9 1.7 divide_convert_fusion
  130.6 1.0 copy.107
  131.6 0.9 broadcast_in_dim.71
  132.5 2.0 reshape.305
  134.5 6.4 %scatter_custom_fusion.1 = bf16[2049,256]{1,0:T(8,128)(2,1)} fusion(s32[1024]{0:T(1024)} %bitcast.75, bf16[1024,256]{1,0:T(8,128)(2,1)} %reshape.305, bf16[]{:T(256)} %constant.117.clone.1), kind=kCustom, calls=%fused_computation.59 | custom fusion | bytes 1049600 | tf_op jit(solution)/shard_map/scatter | solution.py:142
  140.9 2.3 slice.22
  143.2 5.8 %all-to-all-start.2 = ((bf16[8,256,256]{2,1,0:T(8,128)(2,1)}), bf16[8,256,256]{2,1,0:T(8,128)(2,1)}, u32[]{:S(2)}, u32[]{:S(2)}) async-start(bf16[8,256,256]{2,1,0:T(8,128)(2,1)} %bitcast.65), calls=%async_computation.2 | async-start | bytes 2097152 | tf_op jit(solution)/shard_map/all_to_all | solution.py:144
  149.1 1.8 fusion.62
  150.9 0.2 reduce-scatter.2.cloned.1.call-start
  151.2 25.7 %all-to-all-done.2 = bf16[8,256,256]{2,1,0:T(8,128)(2,1)} async-done(((bf16[8,256,256]{2,1,0:T(8,128)(2,1)}), bf16[8,256,256]{2,1,0:T(8,128)(2,1)}, u32[]{:S(2)}, u32[]{:S(2)}) %all-to-all-start.2) | async-done | bytes 1048608 | tf_op jit(solution)/shard_map/all_to_all | solution.py:144
  176.9 15.7 %scatter_custom_fusion.2 = f32[2048,256]{1,0:T(8,128)} fusion(s32[2048]{0:T(1024)S(1)} %bitcast.73, bf16[2048,256]{1,0:T(8,128)(2,1)} %bitcast.17, f32[]{:T(128)} %constant.116.clone.1), kind=kCustom, calls=%fused_computation.53 | custom fusion | flops 1048576 | bytes 3145732 | tf_op jit(solution)/shard_map/scatter-add | solution.py:148
  192.8 11.8 %all_gather.6 = bf16[1024,256]{0,1:T(8,128)(2,1)S(1)} all-gather(bf16[256,256]{0,1:T(8,128)(2,1)S(1)} %copy-done.1), channel_id=1, replica_groups=mesh['shard'=8,'blk'=4] {'blk'}, dimensions={0}, use_global_device_ids=true | all-gather | bytes 655360 | tf_op jit(solution)/shard_map/all_gather | solution.py:87
  204.6 7.5 %while.28 = (s32[]{:T(128)}, f32[256,256]{1,0:T(8,128)S(1)}, f32[]{:T(128)}, bf16[1024,256]{0,1:T(8,128)(2,1)S(1)}, bf16[256,256]{1,0:T(8,128)(2,1)S(1)}, /*inde...) while((s32[]{:T(128)}, f32[256,256]{1,0:T(8,128)S(1)}, ...), condition=%wide.region_9.10_spmd.clone, body=%wide.region_8.9_spmd.clone.sunk | while | flops 67830280 | bytes 923316 | solution.py:99
  204.6 1.8 convolution_add_fusion.5
  206.4 1.8 convolution_add_fusion.5
  208.3 1.8 convolution_add_fusion.5
  210.2 1.8 convolution_add_fusion.5
  212.0 0.1 copy.103
  212.3 0.8 copy.108
  213.2 88.6 %all-reduce.2.cloned.1.call-done = f32[2048,256]{1,0:T(8,128)} async-done(((f32[2048,256]{1,0:T(8,128)}), f32[2048,256]{1,0:T(8,128)}) %all-reduce.2.cloned.1.call-update) | async-done | bytes 2097168 | tf_op jit(solution)/shard_map/psum | solution.py:150
  301.7 3.0 copy.131
  (64 shorter events, 1.3 us)
Async XLA Ops:
  8.0 24.1 %copy-start = (f32[2048,256]{1,0:T(8,128)S(1)}, f32[2048,256]{1,0:T(8,128)}, u32[]{:S(2)}) copy-start(f32[2048,256]{1,0:T(8,128)} %param.15) | copy-start | bytes 6291460
  16.2 24.5 %copy-start.12 = (s32[1024,1]{0,1:T(1,128)}, s32[1024,1]{0,1:T(1,128)S(1)}, u32[]{:S(2)}) copy-start(s32[1024,1]{0,1:T(1,128)S(1)} %get-tuple-element.442) | copy-start | bytes 12292
  44.0 4.7 %copy-start.6 = (s32[256,4]{0,1:T(4,128)S(1)}, s32[256,4]{0,1:T(4,128)}, u32[]{:S(2)}) copy-start(s32[256,4]{0,1:T(4,128)} %param.17) | copy-start | bytes 12292
  44.0 4.7 %copy-start.10 = (s32[256]{0:T(256)S(1)}, s32[256]{0:T(256)}, u32[]{:S(2)}) copy-start(s32[256]{0:T(256)} %param.19) | copy-start | bytes 3076
  44.0 6.3 %copy-start.5 = (bf16[256,256]{1,0:T(8,128)(2,1)S(1)}, bf16[256,256]{1,0:T(8,128)(2,1)}, u32[]{:S(2)}) copy-start(bf16[256,256]{1,0:T(8,128)(2,1)} %param.13) | copy-start | bytes 393220
  44.0 17.9 %copy-start.11 = (s32[256,4]{0,1:T(4,128)S(1)}, s32[256,4]{0,1:T(4,128)}, u32[]{:S(2)}) copy-start(s32[256,4]{0,1:T(4,128)} %param.16) | copy-start | bytes 12292
  44.0 50.7 %all-to-all-start.1 = ((f32[8,256,256]{2,1,0:T(8,128)}), f32[8,256,256]{2,1,0:T(8,128)}, u32[]{:S(2)}, u32[]{:S(2)}) async-start(f32[8,256,256]{2,1,0:T(8,128)} %broadcast_select_fusion), calls=%async_computation.1 | async-start | bytes 4194304 | tf_op jit(solution)/shard_map/all_to_all | solution.py:53
  51.2 0.6 copy-start.7
  51.7 0.6 copy-start.2
  108.8 0.6 copy-start.9
  140.9 8.2 %copy-start.4 = (bf16[256,256]{0,1:T(8,128)(2,1)S(1)}, bf16[256,256]{0,1:T(8,128)(2,1)}, u32[]{:S(2)}) copy-start(bf16[256,256]{0,1:T(8,128)(2,1)} %divide_convert_fusion) | copy-start | bytes 393220
  143.2 33.7 %all-to-all-start.2 = ((bf16[8,256,256]{2,1,0:T(8,128)(2,1)}), bf16[8,256,256]{2,1,0:T(8,128)(2,1)}, u32[]{:S(2)}, u32[]{:S(2)}) async-start(bf16[8,256,256]{2,1,0:T(8,128)(2,1)} %bitcast.65), calls=%async_computation.2 | async-start | bytes 2097152 | tf_op jit(solution)/shard_map/all_to_all | solution.py:144
  149.0 152.7 %all-reduce.2.cloned.1.call-start = ((), (), s32[]{:S(2)}) async-start(), calls=%async_computation.4 | async-start | bytes 4194304 | tf_op jit(solution)/shard_map/psum | solution.py:150
  150.9 150.8 %reduce-scatter.2.cloned.1.call-start = ((), (), s32[]{:S(2)}) async-start(), calls=%async_computation.5 | async-start | bytes 2621440 | tf_op jit(solution)/shard_map/reduce_scatter | solution.py:151
  176.9 15.8 %copy-start.3 = (bf16[256,256]{0,1:T(8,128)(2,1)S(1)}, bf16[256,256]{0,1:T(8,128)(2,1)}, u32[]{:S(2)}) copy-start(bf16[256,256]{0,1:T(8,128)(2,1)} %copy-done.2) | copy-start | bytes 393220
  176.9 15.9 %copy-start.1 = (bf16[256,256]{0,1:T(8,128)(2,1)S(1)}, bf16[256,256]{0,1:T(8,128)(2,1)}, u32[]{:S(2)}) copy-start(bf16[256,256]{0,1:T(8,128)(2,1)} %fusion.61) | copy-start | bytes 393220
  204.6 7.6 %copy-start.8 = (f32[256]{0:T(256)S(1)}, f32[256]{0:T(256)}, u32[]{:S(2)}) copy-start(f32[256]{0:T(256)} %copy-done.7) | copy-start | bytes 3076
Sparse Core Ops, SparseCore 0:
  155.8 145.9 all-reduce.1
Sparse Core Ops, SparseCore 1:
  192.7 32.3 reduce-scatter.1
where the time goes:
time: 315 us; the launch traced here: 312 us
  waiting for transfers between devices  146 us (46%)
  local copies, waits for them, and re-layouts  50.5 us (16%)
  blocking collectives  32.9 us (10%)
  other arithmetic  30.4 us (10%)
  matrix products  25.4 us (8%)
  between operations  16.5 us (5%)
  starting transfers between devices  10.6 us (3%)
    psum x1, waiting for transfers between devices, body(): hot_grad = lax.psum(hot_local, ('shard', 'blk'))  88.6 us
    all_to_all x1, waiting for transfers between devices, body(): lax.all_to_all(looked, 'shard', split_axis=0, concat_axis=0, tiled=True)  31.5 us
    all_to_all x1, waiting for transfers between devices, body(): lax.all_to_all(outgoing, 'shard', split_axis=0, concat_axis=0, tiled=True)  25.7 us
    scatter-add x1, other arithmetic, body(): cold_local = jnp.zeros((rare_entry_matrix.shape[0], row_width), jnp.float...  15.7 us
    dot_general x4, matrix products, item_block(): lax.dot_general(pairscore_derivative, query_rows, (((0,), (0,)), ((), ())...  14.4 us
    all_gather x1, blocking collectives, body(): lax.all_gather(candidate_reduced, 'blk', axis=0, tiled=True)  11.8 us
    all_to_all x1, blocking collectives, body(): lax.all_to_all(requests, 'shard', split_axis=0, concat_axis=0, tiled=True)  11.5 us
    all_gather x1, blocking collectives, body(): lax.all_gather(request_reduced, 'blk', axis=0, tiled=True)  9.56 us
  transfers between devices with their start and end apart: 4, of which 3 were waited for; matrix products, arithmetic and copies ran while one was open for 9% of the time, Pallas kernels for 0%

commit v1 on v0

v1 whole, which is shorter than its diff:
```python
import functools

import jax
import jax.numpy as jnp
from jax import lax
from jax.experimental import pallas as pl
from jax.experimental.pallas import tpu as pltpu
from jax.sharding import PartitionSpec as P

epsilon = 1e-06
BF = jnp.bfloat16
F32 = jnp.float32


def normalize_rows(vectors):
    radius = jnp.sqrt(jnp.sum(vectors * vectors, axis=1, keepdims=True) + epsilon)
    return (vectors / radius, radius)


def projection_backward(unit_vectors, radius, gradient):
    inner = jnp.sum(unit_vectors * gradient, axis=1, keepdims=True)
    return (gradient - unit_vectors * inner) / radius


def kernel(
    S,
    B,
    scale_ref,
    bias_ref,
    req_ref,
    hot_ref,
    cold_ref,
    lines_ref,
    parent_ref,
    pos_ref,
    tally_ref,
    dq_ref,
    hotg_ref,
    coldg_ref,
    keys,
    coldb,
    ysend,
    yrecv,
    zsend,
    zrecv,
    queries,
    qsend,
    qrecv,
    qunit,
    qdir,
    grads,
    coldacc,
    csend,
    crecv,
    hotacc,
    hpart,
    hfull,
    sem_ks,
    sem_kr,
    sem_ys,
    sem_yr,
    sem_zs,
    sem_zr,
    sem_qs,
    sem_qr,
    sem_ps,
    sem_pr,
    sem_gz,
    sem_gy,
    sem_gc,
    sem_gr,
    sem_cs,
    sem_cr,
    sem_xs,
    sem_xr,
    sem_hz,
    sem_hy,
    sem_hc,
    sem_hr,
):
    S2, B2, U = S // 2, B // 2, 2 * S
    pairs, width = req_ref.shape
    rows = cold_ref.shape[0]
    hot_rows = hot_ref.shape[0]
    HB = lines_ref.shape[1]
    CB = parent_ref.shape[1]
    RB = rows // B
    HR = hot_rows // U
    s = lax.axis_index("shard")
    b = lax.axis_index("blk")
    line, y = s // 2, lax.rem(s, 2)
    x, c = b // 2, lax.rem(b, 2)
    u = s * 2 + c
    ypart = line * 2 + (1 - y)
    cpart = x * 2 + (1 - c)
    dot = functools.partial(lax.dot_general, preferred_element_type=F32)

    def send(src, dst, ss, rs, sh, bl):
        return pltpu.make_async_remote_copy(
            src_ref=src,
            dst_ref=dst,
            send_sem=ss,
            recv_sem=rs,
            device_id=(sh, bl),
            device_id_type=pl.DeviceIdType.MESH,
        )

    def loop(lo, hi, f):
        def body(i, carry):
            f(i)
            return carry

        lax.fori_loop(lo, hi, body, 0)

    barrier = pltpu.get_barrier_semaphore()

    def greet(k):
        v = lax.rem(u + k, U)
        pl.semaphore_signal(
            barrier,
            inc=1,
            device_id=(v // 2, x * 2 + lax.rem(v, 2)),
            device_id_type=pl.DeviceIdType.MESH,
        )

    loop(1, U, greet)

    def greet_blk(k):
        xo = lax.rem(x + k, B2)
        for cc in range(2):
            pl.semaphore_signal(
                barrier, inc=1, device_id=(s, xo * 2 + cc), device_id_type=pl.DeviceIdType.MESH
            )

    loop(1, B2, greet_blk)

    slot = lax.broadcasted_iota(jnp.int32, (pairs, CB), 1)
    cold_key = jnp.where(slot < tally_ref[...], parent_ref[...] * rows + pos_ref[...], -1)
    both = jnp.concatenate(
        [lines_ref[...], cold_key, jnp.zeros((pairs, 128 - HB - CB), jnp.int32)], axis=1
    )
    keys[u] = jnp.transpose(both)[:8, :]

    qf = req_ref[...].astype(F32)
    q_unit, q_radius = normalize_rows(qf)
    qunit[...] = q_unit
    queries[b] = q_unit.astype(BF)

    pl.semaphore_wait(barrier, U - 1 + 2 * (B2 - 1))

    def key_copy(src_u, k, v):
        return send(
            keys.at[src_u],
            keys.at[src_u],
            sem_ks.at[k],
            sem_kr.at[src_u],
            v // 2,
            x * 2 + lax.rem(v, 2),
        )

    def send_keys(k):
        v = lax.rem(u + k, U)
        key_copy(u, k, v).start()

    loop(1, U, send_keys)

    def q_copy(slot_b, k, bo):
        return send(
            queries.at[slot_b], queries.at[slot_b], sem_qs.at[k], sem_qr.at[slot_b], s, bo
        )

    loop(1, B, lambda k: q_copy(b, k, lax.rem(b + k, B)).start())

    coldb[...] = cold_ref[...].astype(BF)

    def own_index(v):
        block = keys[v]
        rel = block[HB : HB + CB, :] - s * rows
        good = (rel >= 0) & (rel < rows) & (block[HB : HB + CB, :] >= 0)
        return jnp.max(jnp.where(good, rel, -1), axis=0, keepdims=True)

    def lookup(p):
        idx = own_index(p * 2 + c)
        col = jnp.transpose(jnp.broadcast_to(idx, (128, pairs)))[:, :1]
        hit = lax.broadcasted_iota(jnp.int32, (pairs, rows), 1) == col
        return dot(hit.astype(F32).astype(BF), coldb[...], (((1,), (0,)), ((), ())))

    def y_copy(lo):
        return send(ysend.at[lo], yrecv.at[lo], sem_ys.at[lo], sem_yr.at[lo], ypart, b)

    def z_copy(src, dst, lo):
        return send(zsend.at[src], zrecv.at[dst], sem_zs.at[src], sem_zr.at[dst], lo * 2 + y, b)

    def wait_key(v):
        key_copy(v, 0, v).wait_recv()

    def fetch_y(k):
        lo = lax.rem(line + k, S2)
        p = lo * 2 + (1 - y)
        wait_key(p * 2 + c)
        ysend[lo] = lookup(p).astype(BF)
        y_copy(lo).start()

    loop(1, S2 + 1, fetch_y)

    def fetch_z(k):
        lo = lax.rem(line + k, S2)
        p = lo * 2 + y
        wait_key(p * 2 + c)
        part = lookup(p)
        y_copy(lo).wait_recv()
        zsend[lo] = (part + yrecv[lo].astype(F32)).astype(BF)
        z_copy(lo, line, lo).start()

    loop(1, S2, fetch_z)

    lines = lines_ref[...]
    hot_iota = lax.broadcasted_iota(jnp.int32, (pairs, hot_rows), 1)
    counts = jnp.zeros((pairs, hot_rows), F32)
    for h in range(HB):
        counts = counts + (hot_iota == lines[:, h : h + 1]).astype(F32)
    item = dot(counts.astype(BF), hot_ref[...], (((1,), (0,)), ((), ())))
    item = item + lookup(s)
    y_copy(line).wait_recv()
    item = item + yrecv[line].astype(F32)

    def take_z(k, acc):
        lo = lax.rem(line + S2 - k, S2)
        z_copy(line, lo, lo).wait_recv()
        return acc + zrecv[lo].astype(F32)

    item = lax.fori_loop(1, S2, take_z, item)

    unit, radius = normalize_rows(item)
    low = unit.astype(BF)
    scale = scale_ref[0]
    bias = bias_ref[0]
    diag = lax.broadcasted_iota(jnp.int32, (pairs, pairs), 0) == lax.broadcasted_iota(
        jnp.int32, (pairs, pairs), 1
    )

    def pair_grads(q, positive):
        logits = scale * dot(low, q, (((1,), (1,)), ((), ()))) + bias
        g = jax.nn.sigmoid(logits)
        if positive:
            g = g - diag.astype(F32)
        g = g.astype(BF)
        return dot(g, q, (((1,), (0,)), ((), ()))), dot(g, low, (((0,), (0,)), ((), ())))

    item_dir, own_qdir = pair_grads(queries[b], True)
    qdir[...] = own_qdir

    def p_copy(bo, dst):
        return send(qsend.at[bo], qrecv.at[dst], sem_ps.at[bo], sem_pr.at[dst], s, bo)

    def loss_block(k, acc):
        bo = lax.rem(b + k, B)
        q_copy(bo, 0, bo).wait_recv()
        add, part = pair_grads(queries[bo], False)
        qsend[bo] = part.astype(BF)
        p_copy(bo, b).start()
        return acc + add

    item_dir = lax.fori_loop(1, B, loss_block, item_dir)
    grads[u] = projection_backward(unit, radius, scale * item_dir).astype(BF)

    def gz_copy(v, lo):
        return send(grads.at[v], grads.at[v], sem_gz.at[lo], sem_gr.at[v], lo * 2 + y, b)

    def gy_copy(v, lo):
        return send(grads.at[v], grads.at[v], sem_gy.at[lo], sem_gr.at[v], ypart, b)

    def gc_copy(v, p):
        return send(grads.at[v], grads.at[v], sem_gc.at[p], sem_gr.at[v], s, cpart)

    loop(1, S2, lambda k: gz_copy(u, lax.rem(line + k, S2)).start())

    coldacc[...] = jnp.zeros(coldacc.shape, F32)
    hotacc[...] = jnp.zeros(hotacc.shape, F32)
    row_iota = lax.broadcasted_iota(jnp.int32, (RB, pairs), 0)
    hrow_iota = lax.broadcasted_iota(jnp.int32, (HR, pairs), 0) + u * HR

    def consume(v):
        g = grads[v]
        idx = own_index(v)
        block = keys[v]
        cnt = jnp.zeros((HR, pairs), F32)
        for h in range(HB):
            cnt = cnt + (hrow_iota == block[h : h + 1, :]).astype(F32)
        hotacc[...] += dot(cnt.astype(BF), g, (((1,), (0,)), ((), ())))

        def part(xo):
            hit = (row_iota == idx - (xo * 2 + c) * RB).astype(F32).astype(BF)
            coldacc[xo] += dot(hit, g, (((1,), (0,)), ((), ())))

        loop(0, B2, part)

    def own_column(k):
        lo = lax.rem(line + S2 - k, S2)
        p = lo * 2 + y
        v = p * 2 + c

        @pl.when(k > 0)
        def _():
            gz_copy(v, lo).wait_recv()

        gy_copy(v, lo).start()
        gc_copy(v, p).start()
        consume(v)

    loop(0, S2, own_column)

    def y_column(k):
        lo = lax.rem(line + S2 - k, S2)
        p = lo * 2 + (1 - y)
        v = p * 2 + c
        gy_copy(v, lo).wait_recv()
        gc_copy(v, p).start()
        consume(v)

    loop(0, S2, y_column)

    def core_column(k):
        p = lax.rem(s + S - k, S)
        v = p * 2 + (1 - c)
        wait_key(v)
        gc_copy(v, p).wait_recv()
        consume(v)

    loop(0, S, core_column)

    def x_copy(dst, xo):
        return send(
            hpart.at[x], hpart.at[dst], sem_xs.at[xo], sem_xr.at[dst], s, xo * 2 + c
        )

    hpart[x] = hotacc[...].astype(BF)
    loop(1, B2, lambda k: x_copy(x, lax.rem(x + k, B2)).start())

    def c_copy(src, dst):
        return send(
            csend.at[src], crecv.at[dst], sem_cs.at[src], sem_cr.at[dst], s, src * 2 + c
        )

    def send_cold(k):
        xo = lax.rem(x + k, B2)
        csend[xo] = coldacc[xo].astype(BF)
        c_copy(xo, x).start()

    loop(1, B2, send_cold)

    def wait_x(k):
        xo = lax.rem(x + k, B2)
        x_copy(xo, xo).wait_recv()

    loop(1, B2, wait_x)
    total = hpart[0].astype(F32)
    for xo in range(1, B2):
        total = total + hpart[xo].astype(F32)
    hfull[u] = total.astype(BF)

    def hz_copy(v, lo):
        return send(hfull.at[v], hfull.at[v], sem_hz.at[lo], sem_hr.at[v], lo * 2 + y, b)

    def hy_copy(v, lo):
        return send(hfull.at[v], hfull.at[v], sem_hy.at[lo], sem_hr.at[v], ypart, b)

    def hc_copy(v, p):
        return send(hfull.at[v], hfull.at[v], sem_hc.at[p], sem_hr.at[v], s, cpart)

    loop(1, S2, lambda k: hz_copy(u, lax.rem(line + k, S2)).start())
    hy_copy(u, line).start()
    hc_copy(u, s).start()

    def take_p(k, acc):
        bo = lax.rem(b + k, B)
        p_copy(bo, bo).wait_recv()
        return acc + qrecv[bo].astype(F32)

    q_total = lax.fori_loop(1, B, take_p, qdir[...])
    _, q_radius2 = normalize_rows(req_ref[...].astype(F32))
    dq_ref[...] = projection_backward(qunit[...], q_radius2, scale * q_total)

    def hot_line(k):
        lo = lax.rem(line + S2 - k, S2)
        p = lo * 2 + y
        v = p * 2 + c
        hz_copy(v, lo).wait_recv()
        hy_copy(v, lo).start()
        hc_copy(v, p).start()

    loop(1, S2, hot_line)

    def hot_y(k):
        lo = lax.rem(line + S2 - k, S2)
        p = lo * 2 + (1 - y)
        v = p * 2 + c
        hy_copy(v, lo).wait_recv()
        hc_copy(v, p).start()

    loop(0, S2, hot_y)

    def take_cold(k, acc):
        xo = lax.rem(x + k, B2)
        c_copy(xo, xo).wait_recv()
        return acc + crecv[xo].astype(F32)

    coldg_ref[...] = lax.fori_loop(1, B2, take_cold, coldacc[x])

    def hot_core(k):
        p = lax.rem(s + S - k, S)
        hc_copy(p * 2 + (1 - c), p).wait_recv()

    loop(0, S, hot_core)
    hotg_ref[...] = hfull[...]

    loop(1, U, lambda k: key_copy(u, k, lax.rem(u + k, U)).wait_send())
    loop(1, B, lambda k: q_copy(b, k, lax.rem(b + k, B)).wait_send())
    loop(0, S2, lambda lo: y_copy(lo).wait_send())

    def sent_line(k):
        lo = lax.rem(line + k, S2)
        z_copy(lo, line, lo).wait_send()
        gz_copy(u, lo).wait_send()
        hz_copy(u, lo).wait_send()

    loop(1, S2, sent_line)
    loop(1, B, lambda k: p_copy(lax.rem(b + k, B), b).wait_send())

    def sent_y(lo):
        gy_copy((lo * 2 + y) * 2 + c, lo).wait_send()
        hy_copy((lo * 2 + y) * 2 + c, lo).wait_send()

    loop(0, S2, sent_y)

    def sent_c(p):
        gc_copy(p * 2 + c, p).wait_send()
        hc_copy(p * 2 + c, p).wait_send()

    loop(0, S, sent_c)

    def sent_x(k):
        xo = lax.rem(x + k, B2)
        x_copy(x, xo).wait_send()
        c_copy(xo, x).wait_send()

    loop(1, B2, sent_x)


def body(
    request_embeddings,
    frequent_entry_matrix,
    rare_entry_matrix,
    frequent_entry_lines,
    rare_place_parent,
    rare_local_position,
    rare_place_tally,
    sharpness_factor,
    pairscore_additive,
):
    pairs, width = request_embeddings.shape
    S = lax.axis_size("shard")
    B = lax.axis_size("blk")
    rows = rare_entry_matrix.shape[0]
    hot_rows = frequent_entry_matrix.shape[0]
    S2, B2, U = S // 2, B // 2, 2 * S
    RB, HR = rows // B, hot_rows // U
    vmem = pl.BlockSpec(memory_space=pltpu.VMEM)
    smem = pl.BlockSpec(memory_space=pltpu.SMEM)
    dma = lambda n: pltpu.SemaphoreType.DMA((n,))
    blocks = lambda n, dtype: pltpu.VMEM((n, pairs, width), dtype)
    dq, hot, cold = pl.pallas_call(
        functools.partial(kernel, S, B),
        out_shape=(
            jax.ShapeDtypeStruct((pairs, width), F32),
            jax.ShapeDtypeStruct((U, HR, width), BF),
            jax.ShapeDtypeStruct((RB, width), F32),
        ),
        in_specs=[smem, smem] + [vmem] * 7,
        out_specs=(vmem, vmem, vmem),
        scratch_shapes=[
            pltpu.VMEM((U, 8, pairs), jnp.int32),
            pltpu.VMEM((rows, width), BF),
            blocks(S2, BF),
            blocks(S2, BF),
            blocks(S2, BF),
            blocks(S2, BF),
            blocks(B, BF),
            blocks(B, BF),
            blocks(B, BF),
            pltpu.VMEM((pairs, width), F32),
            pltpu.VMEM((pairs, width), F32),
            blocks(U, BF),
            pltpu.VMEM((B2, RB, width), F32),
            pltpu.VMEM((B2, RB, width), BF),
            pltpu.VMEM((B2, RB, width), BF),
            pltpu.VMEM((HR, width), F32),
            pltpu.VMEM((B2, HR, width), BF),
            pltpu.VMEM((U, HR, width), BF),
            dma(U),
            dma(U),
            dma(S2),
            dma(S2),
            dma(S2),
            dma(S2),
            dma(B),
            dma(B),
            dma(B),
            dma(B),
            dma(S2),
            dma(S2),
            dma(S),
            dma(U),
            dma(B2),
            dma(B2),
            dma(B2),
            dma(B2),
            dma(S2),
            dma(S2),
            dma(S),
            dma(U),
        ],
        compiler_params=pltpu.CompilerParams(
            collective_id=0, has_side_effects=True, vmem_limit_bytes=56 * 1024 * 1024
        ),
    )(
        sharpness_factor,
        pairscore_additive,
        request_embeddings,
        frequent_entry_matrix,
        rare_entry_matrix,
        frequent_entry_lines,
        rare_place_parent,
        rare_local_position,
        rare_place_tally.reshape(pairs, 1),
    )
    return dq, hot.reshape(hot_rows, width).astype(F32), cold


def solution(mesh):
    in_specs = (
        P(("shard", "blk"), None),
        P(),
        P("shard", None),
        P(("shard", "blk"), None),
        P(("shard", "blk"), None),
        P(("shard", "blk"), None),
        P(("shard", "blk")),
        P(),
        P(),
    )
    out_specs = (P(("shard", "blk"), None), P(), P(("shard", "blk"), None))
    return jax.shard_map(body, mesh=mesh, in_specs=in_specs, out_specs=out_specs, check_vma=False)
```

time: 315 us -> 88.6 us (0.28)
  waiting for transfers between devices: 146 us -> 0 us
  Pallas kernels: 0 us -> 76.1 us
  local copies, waits for them, and re-layouts: 50.5 us -> 7.42 us
  blocking collectives: 32.9 us -> 0 us
  other arithmetic: 30.4 us -> 2.77 us
  matrix products: 25.4 us -> 0 us
  between operations: 16.5 us -> 1.95 us
  starting transfers between devices: 10.6 us -> 0 us
    psum x1 -> x0, waiting for transfers between devices: 88.6 us -> none  [body(): hot_grad = lax.psum(hot_local, ('shard', 'blk'))]
    pallas_call x0 -> x1, Pallas kernels: none -> 76.1 us  [body(): pl.pallas_call(functools.partial(kernel, S, B), out_shape=(jax.ShapeDtype...]
    all_to_all x2 -> x0, waiting for transfers between devices: 57.2 us -> none  [the longest x1 31.5 us: body(): lax.all_to_all(looked, 'shard', split_axis=0, concat_axis=0, tiled=True)]
    dot_general x10 -> x0, matrix products: 25.4 us -> none  [the longest x4 14.4 us: item_block(): lax.dot_general(pairscore_derivative, query_rows, (((0,), (0,)), ((), ())...]
    all_gather x2 -> x0, blocking collectives: 21.3 us -> none  [the longest x1 11.8 us: body(): lax.all_gather(candidate_reduced, 'blk', axis=0, tiled=True)]
    gather x3 -> x0, local copies, waits for them, and re-layouts: 17.4 us -> none  [the longest x2 8.78 us: body(): jnp.take(fetched_flat, jnp.minimum(bucket, dump_slot - 1), axis=0)]
    scatter-add x1 -> x0, other arithmetic: 15.7 us -> none  [body(): cold_local = jnp.zeros((rare_entry_matrix.shape[0], row_width), jnp.float...]
    all_to_all x1 -> x0, blocking collectives: 11.5 us -> none  [body(): lax.all_to_all(requests, 'shard', split_axis=0, concat_axis=0, tiled=True)]
  transfers between devices with their start and end apart: 4 -> 0, of which waited for: 3 -> 0; matrix products, arithmetic and copies ran while one was open for 9% -> 0% of each run, Pallas kernels for 0% -> 0%
where the time goes in v1:
time: 88.6 us; the launch traced here: 88.3 us
  Pallas kernels  76.1 us (86%)
  local copies, waits for them, and re-layouts  7.42 us (8%)
  other arithmetic  2.77 us (3%)
  between operations  1.95 us (2%)
    pallas_call x1, Pallas kernels, body(): pl.pallas_call(functools.partial(kernel, S, B), out_shape=(jax.ShapeDtype...  76.1 us
    unnamed x9, local copies, waits for them, and re-layouts  5.95 us
    convert_element_type x1, other arithmetic, body(): return (dq, hot.reshape(hot_rows, width).astype(F32), cold)  2.77 us

profile of v1, /device:TPU:1, one launch (start us, length us, event | category | flops | bytes accessed | tf_op | source)
XLA Modules:
  0.0 88.3 jit_solution(4785932885110859372)
XLA Ops:
  1.9 1.5 %copy.15.lines_ref = s32[256,4]{1,0:T(8,128)} copy(s32[256,4]{0,1:T(4,128)} %param.12) | data formatting | bytes 8192 | tf_op args[3]
  3.4 1.5 %copy.16.parent_ref = s32[256,4]{1,0:T(8,128)} copy(s32[256,4]{0,1:T(4,128)} %param.13) | data formatting | bytes 8192 | tf_op args[4]
  4.9 1.5 %copy.17.pos_ref = s32[256,4]{1,0:T(8,128)} copy(s32[256,4]{0,1:T(4,128)} %param.14) | data formatting | bytes 8192 | tf_op args[5]
  6.4 1.5 %copy.18.tally_ref = s32[256,1]{1,0:T(8,128)} copy(s32[256,1]{0,1:T(1,128)} %bitcast.4) | data formatting | bytes 2048 | tf_op jit(solution)/shard_map/reshape | solution.py:535
  7.8 76.1 %shard_map.112 = (f32[256,256]{1,0:T(8,128)}, bf16[16,128,256]{2,1,0:T(8,128)(2,1)}, f32[512,256]{1,0:T(8,128)}) custom-call(f32[1]{0:T(128)S(6)} %copy.21.scale_ref, f32[1]{0:T(128)S(6)} %copy.22.bias_ref, bf16[256,256]{1,0:T(8,128)(2,1)} %req_ref.1, bf16[2048,256]{1,0:T(8,128)(2,1)} %hot_ref.1, f32[2048,256]{1,0:T(8,128)} %cold_ref.1, ...), custom_call_target="tpu_custom_call" | custom-call | tf_op jit(solution)/shard_map/pallas_call | solution.py:472
  84.0 0.0 copy-start.1
  84.0 0.0 copy-start
  84.0 2.8 %bitcast_convert_fusion = f32[2048,256]{1,0:T(8,128)} fusion(bf16[16,128,256]{2,1,0:T(8,128)(2,1)} %get-tuple-element.7), kind=kLoop, calls=%fused_computation | loop fusion | flops 524288 | bytes 3145728 | tf_op jit(solution)/shard_map/convert_element_type | solution.py:537
  86.8 0.0 copy-done.1
  86.8 0.7 copy.23
  87.5 0.0 copy-done
  87.5 0.8 copy.24
Async XLA Ops:
  84.0 2.8 %copy-start.1 = (f32[256,256]{1,0:T(8,128)S(1)}, f32[256,256]{1,0:T(8,128)}, u32[]{:S(2)}) copy-start(f32[256,256]{1,0:T(8,128)} %get-tuple-element.12) | copy-start | bytes 786436
  84.0 3.5 %copy-start = (f32[512,256]{1,0:T(8,128)S(1)}, f32[512,256]{1,0:T(8,128)}, u32[]{:S(2)}) copy-start(f32[512,256]{1,0:T(8,128)} %get-tuple-element.14) | copy-start | bytes 1572868

commit v2 on v1

--- a/solution.py
+++ b/solution.py
@@ -82,8 +82,8 @@
     pairs, width = req_ref.shape
     rows = cold_ref.shape[0]
     hot_rows = hot_ref.shape[0]
-    HB = lines_ref.shape[1]
-    CB = parent_ref.shape[1]
+    HB = lines_ref.shape[0]
+    CB = parent_ref.shape[0]
     RB = rows // B
     HR = hot_rows // U
     s = lax.axis_index("shard")
@@ -91,6 +91,12 @@
     line, y = s // 2, lax.rem(s, 2)
     x, c = b // 2, lax.rem(b, 2)
     u = s * 2 + c
+    G = 4 if S2 % 4 == 0 else 1
+
+    def place(p, cc):
+        return (cc * 2 + lax.rem(p, 2)) * S2 + p // 2
+
+    w = place(s, c)
     ypart = line * 2 + (1 - y)
     cpart = x * 2 + (1 - c)
     dot = functools.partial(lax.dot_general, preferred_element_type=F32)
@@ -134,12 +140,9 @@
 
     loop(1, B2, greet_blk)
 
-    slot = lax.broadcasted_iota(jnp.int32, (pairs, CB), 1)
+    slot = lax.broadcasted_iota(jnp.int32, (CB, pairs), 0)
     cold_key = jnp.where(slot < tally_ref[...], parent_ref[...] * rows + pos_ref[...], -1)
-    both = jnp.concatenate(
-        [lines_ref[...], cold_key, jnp.zeros((pairs, 128 - HB - CB), jnp.int32)], axis=1
-    )
-    keys[u] = jnp.transpose(both)[:8, :]
+    keys[w] = jnp.concatenate([lines_ref[...], cold_key], axis=0)
 
     qf = req_ref[...].astype(F32)
     q_unit, q_radius = normalize_rows(qf)
@@ -148,21 +151,17 @@
 
     pl.semaphore_wait(barrier, U - 1 + 2 * (B2 - 1))
 
-    def key_copy(src_u, k, v):
-        return send(
-            keys.at[src_u],
-            keys.at[src_u],
-            sem_ks.at[k],
-            sem_kr.at[src_u],
-            v // 2,
-            x * 2 + lax.rem(v, 2),
-        )
+    def key_copy(src_w, k, p, cc):
+        return send(keys.at[src_w], keys.at[src_w], sem_ks.at[k], sem_kr.at[src_w], p, x * 2 + cc)
 
     def send_keys(k):
-        v = lax.rem(u + k, U)
-        key_copy(u, k, v).start()
-
-    loop(1, U, send_keys)
+        key_copy(w, k, lax.rem(s + k, S), c).start()
+
+    def send_keys_core(k):
+        key_copy(w, S + k, lax.rem(s + k, S), 1 - c).start()
+
+    loop(1, S, send_keys)
+    loop(0, S, send_keys_core)
 
     def q_copy(slot_b, k, bo):
         return send(
@@ -173,17 +172,20 @@
 
     coldb[...] = cold_ref[...].astype(BF)
 
-    def own_index(v):
-        block = keys[v]
+    def one_hot(where, idx):
+        same = where.astype(jnp.int16) == idx.astype(jnp.int16)
+        return jnp.where(same, jnp.ones((), BF), jnp.zeros((), BF))
+
+    def own_index(block):
         rel = block[HB : HB + CB, :] - s * rows
         good = (rel >= 0) & (rel < rows) & (block[HB : HB + CB, :] >= 0)
         return jnp.max(jnp.where(good, rel, -1), axis=0, keepdims=True)
 
     def lookup(p):
-        idx = own_index(p * 2 + c)
+        idx = own_index(keys[place(p, c)])
         col = jnp.transpose(jnp.broadcast_to(idx, (128, pairs)))[:, :1]
-        hit = lax.broadcasted_iota(jnp.int32, (pairs, rows), 1) == col
-        return dot(hit.astype(F32).astype(BF), coldb[...], (((1,), (0,)), ((), ())))
+        hit = one_hot(lax.broadcasted_iota(jnp.int32, (pairs, rows), 1), col)
+        return dot(hit, coldb[...], (((1,), (0,)), ((), ())))
 
     def y_copy(lo):
         return send(ysend.at[lo], yrecv.at[lo], sem_ys.at[lo], sem_yr.at[lo], ypart, b)
@@ -191,13 +193,13 @@
     def z_copy(src, dst, lo):
         return send(zsend.at[src], zrecv.at[dst], sem_zs.at[src], sem_zr.at[dst], lo * 2 + y, b)
 
-    def wait_key(v):
-        key_copy(v, 0, v).wait_recv()
+    def wait_key(p, cc):
+        key_copy(place(p, cc), 0, p, cc).wait_recv()
 
     def fetch_y(k):
         lo = lax.rem(line + k, S2)
         p = lo * 2 + (1 - y)
-        wait_key(p * 2 + c)
+        wait_key(p, c)
         ysend[lo] = lookup(p).astype(BF)
         y_copy(lo).start()
 
@@ -206,7 +208,7 @@
     def fetch_z(k):
         lo = lax.rem(line + k, S2)
         p = lo * 2 + y
-        wait_key(p * 2 + c)
+        wait_key(p, c)
         part = lookup(p)
         y_copy(lo).wait_recv()
         zsend[lo] = (part + yrecv[lo].astype(F32)).astype(BF)
@@ -214,12 +216,13 @@
 
     loop(1, S2, fetch_z)
 
-    lines = lines_ref[...]
+    own_keys = jnp.concatenate([keys[w]] * (128 // (HB + CB)), axis=0)
+    lines = jnp.transpose(own_keys)
     hot_iota = lax.broadcasted_iota(jnp.int32, (pairs, hot_rows), 1)
-    counts = jnp.zeros((pairs, hot_rows), F32)
+    counts = jnp.zeros((pairs, hot_rows), BF)
     for h in range(HB):
-        counts = counts + (hot_iota == lines[:, h : h + 1]).astype(F32)
-    item = dot(counts.astype(BF), hot_ref[...], (((1,), (0,)), ((), ())))
+        counts = counts + one_hot(hot_iota, lines[:, h : h + 1])
+    item = dot(counts, hot_ref[...], (((1,), (0,)), ((), ())))
     item = item + lookup(s)
     y_copy(line).wait_recv()
     item = item + yrecv[line].astype(F32)
@@ -262,7 +265,7 @@
         return acc + add
 
     item_dir = lax.fori_loop(1, B, loss_block, item_dir)
-    grads[u] = projection_backward(unit, radius, scale * item_dir).astype(BF)
+    grads[w] = projection_backward(unit, radius, scale * item_dir).astype(BF)
 
     def gz_copy(v, lo):
         return send(grads.at[v], grads.at[v], sem_gz.at[lo], sem_gr.at[v], lo * 2 + y, b)
@@ -273,61 +276,76 @@
     def gc_copy(v, p):
         return send(grads.at[v], grads.at[v], sem_gc.at[p], sem_gr.at[v], s, cpart)
 
-    loop(1, S2, lambda k: gz_copy(u, lax.rem(line + k, S2)).start())
+    loop(1, S2, lambda k: gz_copy(w, lax.rem(line + k, S2)).start())
+    gy_copy(w, line).start()
+    gc_copy(w, s).start()
 
     coldacc[...] = jnp.zeros(coldacc.shape, F32)
     hotacc[...] = jnp.zeros(hotacc.shape, F32)
-    row_iota = lax.broadcasted_iota(jnp.int32, (RB, pairs), 0)
-    hrow_iota = lax.broadcasted_iota(jnp.int32, (HR, pairs), 0) + u * HR
-
-    def consume(v):
-        g = grads[v]
-        idx = own_index(v)
-        block = keys[v]
-        cnt = jnp.zeros((HR, pairs), F32)
-        for h in range(HB):
-            cnt = cnt + (hrow_iota == block[h : h + 1, :]).astype(F32)
-        hotacc[...] += dot(cnt.astype(BF), g, (((1,), (0,)), ((), ())))
-
-        def part(xo):
-            hit = (row_iota == idx - (xo * 2 + c) * RB).astype(F32).astype(BF)
-            coldacc[xo] += dot(hit, g, (((1,), (0,)), ((), ())))
-
-        loop(0, B2, part)
-
-    def own_column(k):
+    row_iota = lax.broadcasted_iota(jnp.int32, (RB, G * pairs), 0)
+    hrow_iota = lax.broadcasted_iota(jnp.int32, (HR, G * pairs), 0)
+
+    def group_rows(first):
+        return jnp.concatenate([grads[first + i] for i in range(G)], axis=0)
+
+    def add_hot(group):
+        def chunk(i):
+            first = group * S2 + i * G
+            ids = jnp.concatenate([keys[first + j][:HB, :] for j in range(G)], axis=1) - u * HR
+            ids = jnp.where((ids >= 0) & (ids < HR), ids, -1)
+            cnt = jnp.zeros((HR, G * pairs), BF)
+            for h in range(HB):
+                cnt = cnt + one_hot(hrow_iota, ids[h : h + 1, :])
+            hotacc[...] += dot(cnt, group_rows(first), (((1,), (0,)), ((), ())))
+
+        loop(0, S2 // G, chunk)
+
+    def add_cold(group, xo):
+        def chunk(i):
+            first = group * S2 + i * G
+            ids = jnp.concatenate([own_index(keys[first + j]) for j in range(G)], axis=1)
+            hit = one_hot(row_iota, ids - (xo * 2 + c) * RB)
+            coldacc[xo] += dot(hit, group_rows(first), (((1,), (0,)), ((), ())))
+
+        loop(0, S2 // G, chunk)
+
+    def line_column(k):
         lo = lax.rem(line + S2 - k, S2)
         p = lo * 2 + y
-        v = p * 2 + c
-
-        @pl.when(k > 0)
-        def _():
-            gz_copy(v, lo).wait_recv()
-
+        v = place(p, c)
+        gz_copy(v, lo).wait_recv()
         gy_copy(v, lo).start()
         gc_copy(v, p).start()
-        consume(v)
-
-    loop(0, S2, own_column)
+
+    loop(1, S2, line_column)
+    mine, other = c * 2, (1 - c) * 2
+    add_hot(mine + y)
+    loop(0, B2, lambda xo: add_cold(mine + y, xo))
 
     def y_column(k):
         lo = lax.rem(line + S2 - k, S2)
         p = lo * 2 + (1 - y)
-        v = p * 2 + c
+        v = place(p, c)
         gy_copy(v, lo).wait_recv()
         gc_copy(v, p).start()
-        consume(v)
 
     loop(0, S2, y_column)
 
-    def core_column(k):
-        p = lax.rem(s + S - k, S)
-        v = p * 2 + (1 - c)
-        wait_key(v)
-        gc_copy(v, p).wait_recv()
-        consume(v)
-
-    loop(0, S, core_column)
+    def core_column(yy):
+        def one(k):
+            p = lax.rem(line + S2 - k, S2) * 2 + yy
+            wait_key(p, 1 - c)
+            gc_copy(place(p, 1 - c), p).wait_recv()
+
+        loop(0, S2, one)
+
+    core_column(y)
+    for group in (other + y, mine + 1 - y):
+        add_hot(group)
+        loop(0, B2, functools.partial(add_cold, group))
+    core_column(1 - y)
+    last = other + 1 - y
+    add_hot(last)
 
     def x_copy(dst, xo):
         return send(
@@ -344,6 +362,7 @@
 
     def send_cold(k):
         xo = lax.rem(x + k, B2)
+        add_cold(last, xo)
         csend[xo] = coldacc[xo].astype(BF)
         c_copy(xo, x).start()
 
@@ -371,6 +390,8 @@
     loop(1, S2, lambda k: hz_copy(u, lax.rem(line + k, S2)).start())
     hy_copy(u, line).start()
     hc_copy(u, s).start()
+
+    add_cold(last, x)
 
     def take_p(k, acc):
         bo = lax.rem(b + k, B)
@@ -414,27 +435,28 @@
     loop(0, S, hot_core)
     hotg_ref[...] = hfull[...]
 
-    loop(1, U, lambda k: key_copy(u, k, lax.rem(u + k, U)).wait_send())
+    loop(1, S, lambda k: key_copy(w, k, lax.rem(s + k, S), c).wait_send())
+    loop(0, S, lambda k: key_copy(w, S + k, lax.rem(s + k, S), 1 - c).wait_send())
     loop(1, B, lambda k: q_copy(b, k, lax.rem(b + k, B)).wait_send())
     loop(0, S2, lambda lo: y_copy(lo).wait_send())
 
     def sent_line(k):
         lo = lax.rem(line + k, S2)
         z_copy(lo, line, lo).wait_send()
-        gz_copy(u, lo).wait_send()
+        gz_copy(w, lo).wait_send()
         hz_copy(u, lo).wait_send()
 
     loop(1, S2, sent_line)
     loop(1, B, lambda k: p_copy(lax.rem(b + k, B), b).wait_send())
 
     def sent_y(lo):
-        gy_copy((lo * 2 + y) * 2 + c, lo).wait_send()
+        gy_copy(place(lo * 2 + y, c), lo).wait_send()
         hy_copy((lo * 2 + y) * 2 + c, lo).wait_send()
 
     loop(0, S2, sent_y)
 
     def sent_c(p):
-        gc_copy(p * 2 + c, p).wait_send()
+        gc_copy(place(p, c), p).wait_send()
         hc_copy(p * 2 + c, p).wait_send()
 
     loop(0, S, sent_c)
@@ -465,6 +487,7 @@
     hot_rows = frequent_entry_matrix.shape[0]
     S2, B2, U = S // 2, B // 2, 2 * S
     RB, HR = rows // B, hot_rows // U
+    ids = frequent_entry_lines.shape[1] + rare_place_parent.shape[1]
     vmem = pl.BlockSpec(memory_space=pltpu.VMEM)
     smem = pl.BlockSpec(memory_space=pltpu.SMEM)
     dma = lambda n: pltpu.SemaphoreType.DMA((n,))
@@ -479,7 +502,7 @@
         in_specs=[smem, smem] + [vmem] * 7,
         out_specs=(vmem, vmem, vmem),
         scratch_shapes=[
-            pltpu.VMEM((U, 8, pairs), jnp.int32),
+            pltpu.VMEM((U, ids, pairs), jnp.int32),
             pltpu.VMEM((rows, width), BF),
             blocks(S2, BF),
             blocks(S2, BF),
@@ -529,10 +552,10 @@
         request_embeddings,
         frequent_entry_matrix,
         rare_entry_matrix,
-        frequent_entry_lines,
-        rare_place_parent,
-        rare_local_position,
-        rare_place_tally.reshape(pairs, 1),
+        frequent_entry_lines.T,
+        rare_place_parent.T,
+        rare_local_position.T,
+        rare_place_tally.reshape(1, pairs),
     )
     return dq, hot.reshape(hot_rows, width).astype(F32), cold
 

time: 88.6 us -> 76.3 us (0.86)
  Pallas kernels: 76.1 us -> 69.9 us
  local copies, waits for them, and re-layouts: 7.42 us -> 1.5 us
    pallas_call x1, Pallas kernels: 76.1 us -> 69.9 us  [body(): pl.pallas_call(functools.partial(kernel, S, B), out_shape=(jax.ShapeDtype...]
    unnamed x9 -> x6, local copies, waits for them, and re-layouts: 5.95 us -> 1.5 us
    reshape x1 -> x0, local copies, waits for them, and re-layouts: 1.47 us -> none  [body(): rare_place_tally.reshape(pairs, 1)]
where the time goes in v2:
time: 76.3 us; the launch traced here: 76.1 us
  Pallas kernels  69.9 us (92%)
  other arithmetic  2.77 us (4%)
  between operations  1.95 us (3%)
  local copies, waits for them, and re-layouts  1.5 us (2%)
    pallas_call x1, Pallas kernels, body(): pl.pallas_call(functools.partial(kernel, S, B), out_shape=(jax.ShapeDtype...  69.9 us
    convert_element_type x1, other arithmetic, body(): return (dq, hot.reshape(hot_rows, width).astype(F32), cold)  2.77 us

profile of v2, /device:TPU:1, one launch (start us, length us, event | category | flops | bytes accessed | tf_op | source)
XLA Modules:
  0.0 76.1 jit_solution(6186850805984196177)
XLA Ops:
  1.9 69.9 %shard_map.112 = (f32[256,256]{1,0:T(8,128)}, bf16[16,128,256]{2,1,0:T(8,128)(2,1)}, f32[512,256]{1,0:T(8,128)}) custom-call(f32[1]{0:T(128)S(6)} %copy.14.scale_ref, f32[1]{0:T(128)S(6)} %copy.15.bias_ref, bf16[256,256]{1,0:T(8,128)(2,1)} %req_ref.1, bf16[2048,256]{1,0:T(8,128)(2,1)} %hot_ref.1, f32[2048,256]{1,0:T(8,128)} %cold_ref.1, s32[4,256]{1,0:T(4,128)} %bitcast.7, ...), custom_call_target="tpu_custom_call" | custom-call | tf_op jit(solution)/shard_map/pallas_call | solution.py:495
  71.8 0.0 copy-start.1
  71.8 0.0 copy-start
  71.8 2.8 %bitcast_convert_fusion = f32[2048,256]{1,0:T(8,128)} fusion(bf16[16,128,256]{2,1,0:T(8,128)(2,1)} %get-tuple-element.7), kind=kLoop, calls=%fused_computation | loop fusion | flops 524288 | bytes 3145728 | tf_op jit(solution)/shard_map/convert_element_type | solution.py:560
  74.6 0.0 copy-done.1
  74.6 0.7 copy.16
  75.3 0.0 copy-done
  75.3 0.8 %copy.17 = f32[512,256]{1,0:T(8,128)} copy(f32[512,256]{1,0:T(8,128)S(1)} %copy-done) | data formatting | bytes 1048576
Async XLA Ops:
  71.8 2.8 %copy-start.1 = (f32[256,256]{1,0:T(8,128)S(1)}, f32[256,256]{1,0:T(8,128)}, u32[]{:S(2)}) copy-start(f32[256,256]{1,0:T(8,128)} %get-tuple-element.12) | copy-start | bytes 786436
  71.8 3.5 %copy-start = (f32[512,256]{1,0:T(8,128)S(1)}, f32[512,256]{1,0:T(8,128)}, u32[]{:S(2)}) copy-start(f32[512,256]{1,0:T(8,128)} %get-tuple-element.14) | copy-start | bytes 1572868

commit v3 on v2

--- a/solution.py
+++ b/solution.py
@@ -267,8 +267,15 @@
     item_dir = lax.fori_loop(1, B, loss_block, item_dir)
     grads[w] = projection_backward(unit, radius, scale * item_dir).astype(BF)
 
-    def gz_copy(v, lo):
-        return send(grads.at[v], grads.at[v], sem_gz.at[lo], sem_gr.at[v], lo * 2 + y, b)
+    def gz_copy(v, lo, way):
+        return send(
+            grads.at[v],
+            grads.at[v],
+            sem_gz.at[(way + 1) // 2 * S2 + lo],
+            sem_gr.at[v],
+            (line + way) * 2 + y,
+            b,
+        )
 
     def gy_copy(v, lo):
         return send(grads.at[v], grads.at[v], sem_gy.at[lo], sem_gr.at[v], ypart, b)
@@ -276,7 +283,37 @@
     def gc_copy(v, p):
         return send(grads.at[v], grads.at[v], sem_gc.at[p], sem_gr.at[v], s, cpart)
 
-    loop(1, S2, lambda k: gz_copy(w, lax.rem(line + k, S2)).start())
+    def hop(copy, lo, v, way, act):
+        ahead = line + way
+
+        @pl.when((ahead >= 0) & (ahead < S2))
+        def _():
+            act(copy(v, lo, way))
+
+    def from_line(wait, d):
+        for way in (1, -1):
+            lo = line - way * d
+
+            @pl.when((lo >= 0) & (lo < S2))
+            def _():
+                wait(lo, way)
+
+    def sent_hops(copy, block_of):
+        def right(lo):
+            @pl.when((lo <= line) & (line + 1 < S2))
+            def _():
+                copy(block_of(lo), lo, 1).wait_send()
+
+        def left(lo):
+            @pl.when((lo >= line) & (line > 0))
+            def _():
+                copy(block_of(lo), lo, -1).wait_send()
+
+        loop(0, S2, right)
+        loop(0, S2, left)
+
+    for way in (1, -1):
+        hop(gz_copy, line, w, way, lambda d: d.start())
     gy_copy(w, line).start()
     gc_copy(w, s).start()
 
@@ -309,15 +346,15 @@
 
         loop(0, S2 // G, chunk)
 
-    def line_column(k):
-        lo = lax.rem(line + S2 - k, S2)
+    def line_column(lo, way):
         p = lo * 2 + y
         v = place(p, c)
-        gz_copy(v, lo).wait_recv()
+        gz_copy(v, lo, -way).wait_recv()
+        hop(gz_copy, lo, v, way, lambda d: d.start())
         gy_copy(v, lo).start()
         gc_copy(v, p).start()
 
-    loop(1, S2, line_column)
+    loop(1, S2, functools.partial(from_line, line_column))
     mine, other = c * 2, (1 - c) * 2
     add_hot(mine + y)
     loop(0, B2, lambda xo: add_cold(mine + y, xo))
@@ -378,8 +415,15 @@
         total = total + hpart[xo].astype(F32)
     hfull[u] = total.astype(BF)
 
-    def hz_copy(v, lo):
-        return send(hfull.at[v], hfull.at[v], sem_hz.at[lo], sem_hr.at[v], lo * 2 + y, b)
+    def hz_copy(v, lo, way):
+        return send(
+            hfull.at[v],
+            hfull.at[v],
+            sem_hz.at[(way + 1) // 2 * S2 + lo],
+            sem_hr.at[v],
+            (line + way) * 2 + y,
+            b,
+        )
 
     def hy_copy(v, lo):
         return send(hfull.at[v], hfull.at[v], sem_hy.at[lo], sem_hr.at[v], ypart, b)
@@ -387,30 +431,20 @@
     def hc_copy(v, p):
         return send(hfull.at[v], hfull.at[v], sem_hc.at[p], sem_hr.at[v], s, cpart)
 
-    loop(1, S2, lambda k: hz_copy(u, lax.rem(line + k, S2)).start())
+    for way in (1, -1):
+        hop(hz_copy, line, u, way, lambda d: d.start())
     hy_copy(u, line).start()
     hc_copy(u, s).start()
 
-    add_cold(last, x)
-
-    def take_p(k, acc):
-        bo = lax.rem(b + k, B)
-        p_copy(bo, bo).wait_recv()
-        return acc + qrecv[bo].astype(F32)
-
-    q_total = lax.fori_loop(1, B, take_p, qdir[...])
-    _, q_radius2 = normalize_rows(req_ref[...].astype(F32))
-    dq_ref[...] = projection_backward(qunit[...], q_radius2, scale * q_total)
-
-    def hot_line(k):
-        lo = lax.rem(line + S2 - k, S2)
+    def hot_line(lo, way):
         p = lo * 2 + y
         v = p * 2 + c
-        hz_copy(v, lo).wait_recv()
+        hz_copy(v, lo, -way).wait_recv()
+        hop(hz_copy, lo, v, way, lambda d: d.start())
         hy_copy(v, lo).start()
         hc_copy(v, p).start()
 
-    loop(1, S2, hot_line)
+    loop(1, S2, functools.partial(from_line, hot_line))
 
     def hot_y(k):
         lo = lax.rem(line + S2 - k, S2)
@@ -421,6 +455,17 @@
 
     loop(0, S2, hot_y)
 
+    add_cold(last, x)
+
+    def take_p(k, acc):
+        bo = lax.rem(b + k, B)
+        p_copy(bo, bo).wait_recv()
+        return acc + qrecv[bo].astype(F32)
+
+    q_total = lax.fori_loop(1, B, take_p, qdir[...])
+    _, q_radius2 = normalize_rows(req_ref[...].astype(F32))
+    dq_ref[...] = projection_backward(qunit[...], q_radius2, scale * q_total)
+
     def take_cold(k, acc):
         xo = lax.rem(x + k, B2)
         c_copy(xo, xo).wait_recv()
@@ -443,10 +488,10 @@
     def sent_line(k):
         lo = lax.rem(line + k, S2)
         z_copy(lo, line, lo).wait_send()
-        gz_copy(w, lo).wait_send()
-        hz_copy(u, lo).wait_send()
 
     loop(1, S2, sent_line)
+    sent_hops(gz_copy, lambda lo: place(lo * 2 + y, c))
+    sent_hops(hz_copy, lambda lo: (lo * 2 + y) * 2 + c)
     loop(1, B, lambda k: p_copy(lax.rem(b + k, B), b).wait_send())
 
     def sent_y(lo):
@@ -530,7 +575,7 @@
             dma(B),
             dma(B),
             dma(B),
-            dma(S2),
+            dma(2 * S2),
             dma(S2),
             dma(S),
             dma(U),
@@ -538,7 +583,7 @@
             dma(B2),
             dma(B2),
             dma(B2),
-            dma(S2),
+            dma(2 * S2),
             dma(S2),
             dma(S),
             dma(U),

time: 76.3 us -> 77.5 us (1.016)
  Pallas kernels: 69.9 us -> 70.9 us
    pallas_call x1, Pallas kernels: 69.9 us -> 70.9 us  [body(): pl.pallas_call(functools.partial(kernel, S, B), out_shape=(jax.ShapeDtype...]
where the time goes in v3:
time: 77.5 us; the launch traced here: 77.2 us
  Pallas kernels  70.9 us (91%)
  other arithmetic  2.77 us (4%)
  between operations  1.95 us (3%)
  local copies, waits for them, and re-layouts  1.5 us (2%)
    pallas_call x1, Pallas kernels, body(): pl.pallas_call(functools.partial(kernel, S, B), out_shape=(jax.ShapeDtype...  70.9 us
    convert_element_type x1, other arithmetic, body(): return (dq, hot.reshape(hot_rows, width).astype(F32), cold)  2.77 us

profile of v3, /device:TPU:1, one launch (start us, length us, event | category | flops | bytes accessed | tf_op | source)
XLA Modules:
  0.0 77.2 jit_solution(11973070328876379289)
XLA Ops:
  1.9 70.9 %shard_map.112 = (f32[256,256]{1,0:T(8,128)}, bf16[16,128,256]{2,1,0:T(8,128)(2,1)}, f32[512,256]{1,0:T(8,128)}) custom-call(f32[1]{0:T(128)S(6)} %copy.14.scale_ref, f32[1]{0:T(128)S(6)} %copy.15.bias_ref, bf16[256,256]{1,0:T(8,128)(2,1)} %req_ref.1, bf16[2048,256]{1,0:T(8,128)(2,1)} %hot_ref.1, f32[2048,256]{1,0:T(8,128)} %cold_ref.1, s32[4,256]{1,0:T(4,128)} %bitcast.7, ...), custom_call_target="tpu_custom_call" | custom-call | tf_op jit(solution)/shard_map/pallas_call | solution.py:540
  72.9 0.0 copy-start.1
  72.9 0.0 copy-start
  72.9 2.8 %bitcast_convert_fusion = f32[2048,256]{1,0:T(8,128)} fusion(bf16[16,128,256]{2,1,0:T(8,128)(2,1)} %get-tuple-element.7), kind=kLoop, calls=%fused_computation | loop fusion | flops 524288 | bytes 3145728 | tf_op jit(solution)/shard_map/convert_element_type | solution.py:605
  75.7 0.0 copy-done.1
  75.7 0.7 copy.16
  76.4 0.0 copy-done
  76.4 0.8 %copy.17 = f32[512,256]{1,0:T(8,128)} copy(f32[512,256]{1,0:T(8,128)S(1)} %copy-done) | data formatting | bytes 1048576
Async XLA Ops:
  72.9 2.8 %copy-start.1 = (f32[256,256]{1,0:T(8,128)S(1)}, f32[256,256]{1,0:T(8,128)}, u32[]{:S(2)}) copy-start(f32[256,256]{1,0:T(8,128)} %get-tuple-element.12) | copy-start | bytes 786436
  72.9 3.5 %copy-start = (f32[512,256]{1,0:T(8,128)S(1)}, f32[512,256]{1,0:T(8,128)}, u32[]{:S(2)}) copy-start(f32[512,256]{1,0:T(8,128)} %get-tuple-element.14) | copy-start | bytes 1572868

commit v4 on v2

--- a/solution.py
+++ b/solution.py
@@ -544,7 +544,7 @@
             dma(U),
         ],
         compiler_params=pltpu.CompilerParams(
-            collective_id=0, has_side_effects=True, vmem_limit_bytes=56 * 1024 * 1024
+            collective_id=0, has_side_effects=True, vmem_limit_bytes=(20 + 4 * S // 4) * 1024 * 1024
         ),
     )(
         sharpness_factor,

time: 76.3 us -> 78.4 us (1.028)
  local copies, waits for them, and re-layouts: 1.5 us -> 7.94 us
  Pallas kernels: 69.9 us -> 66.6 us
  other arithmetic: 2.77 us -> 1.55 us
    unnamed x6 -> x16, local copies, waits for them, and re-layouts: 1.5 us -> 7.94 us
    pallas_call x1, Pallas kernels: 69.9 us -> 66.6 us  [body(): pl.pallas_call(functools.partial(kernel, S, B), out_shape=(jax.ShapeDtype...]
    convert_element_type x1, other arithmetic: 2.77 us -> 1.55 us  [body(): return (dq, hot.reshape(hot_rows, width).astype(F32), cold)]
where the time goes in v4:
time: 78.4 us; the launch traced here: 78.1 us
  Pallas kernels  66.6 us (85%)
  local copies, waits for them, and re-layouts  7.94 us (10%)
  between operations  1.95 us (2%)
  other arithmetic  1.55 us (2%)
    pallas_call x1, Pallas kernels, body(): pl.pallas_call(functools.partial(kernel, S, B), out_shape=(jax.ShapeDtype...  66.6 us
    unnamed x16, local copies, waits for them, and re-layouts  7.94 us

profile of v4, /device:TPU:1, one launch (start us, length us, event | category | flops | bytes accessed | tf_op | source)
XLA Modules:
  0.0 78.1 jit_solution(5817944429776446381)
XLA Ops:
  1.9 0.0 copy-start
  1.9 1.6 %copy-done = f32[2048,256]{1,0:T(8,128)S(1)} copy-done((f32[2048,256]{1,0:T(8,128)S(1)}, f32[2048,256]{1,0:T(8,128)}, u32[]{:S(2)}) %copy-start) | copy-done | bytes 2097176
  3.5 0.0 copy-start.1
  3.5 1.2 %copy-done.1 = bf16[2048,256]{1,0:T(8,128)(2,1)S(1)} copy-done((bf16[2048,256]{1,0:T(8,128)(2,1)S(1)}, bf16[2048,256]{1,0:T(8,128)(2,1)}, u32[]{:S(2)}) %copy-start.1) | copy-done | bytes 1048600
  4.7 0.0 copy-start.2
  4.7 0.9 %copy-done.2 = bf16[256,256]{1,0:T(8,128)(2,1)S(1)} copy-done((bf16[256,256]{1,0:T(8,128)(2,1)S(1)}, bf16[256,256]{1,0:T(8,128)(2,1)}, u32[]{:S(2)}) %copy-start.2) | copy-done | bytes 131096
  5.6 0.0 copy-start.3
  5.6 0.7 copy-done.3
  6.3 0.0 copy-start.4
  6.3 0.7 copy-done.4
  7.0 0.0 copy-start.5
  7.0 0.7 copy-done.5
  7.7 0.0 copy-start.6
  7.7 0.7 copy-done.6
  8.4 66.6 %shard_map.112 = (f32[256,256]{1,0:T(8,128)S(1)}, bf16[16,128,256]{2,1,0:T(8,128)(2,1)S(1)}, f32[512,256]{1,0:T(8,128)S(1)}) custom-call(f32[1]{0:T(128)S(6)} %copy.14.scale_ref, f32[1]{0:T(128)S(6)} %copy.15.bias_ref, bf16[256,256]{1,0:T(8,128)(2,1)S(1)} %copy-done.2, bf16[2048,256]{1,0:T(8,128)(2,1)S(1)} %copy-done.1, f32[2048,256]{1,0:T(8,128)S(1)} %copy-done, ...), custom_call_target="tpu_custom_call" | custom-call | tf_op jit(solution)/shard_map/pallas_call | solution.py:495
  75.0 1.5 %bitcast_convert_fusion = f32[2048,256]{1,0:T(8,128)} fusion(bf16[16,128,256]{2,1,0:T(8,128)(2,1)S(1)} %get-tuple-element.7), kind=kLoop, calls=%fused_computation | loop fusion | flops 524288 | bytes 3145728 | tf_op jit(solution)/shard_map/convert_element_type | solution.py:560
  76.6 0.7 copy.16
  77.3 0.8 %copy.17 = f32[512,256]{1,0:T(8,128)} copy(f32[512,256]{1,0:T(8,128)S(1)} %get-tuple-element.14) | data formatting | bytes 1048576
Async XLA Ops:
  1.9 1.6 %copy-start = (f32[2048,256]{1,0:T(8,128)S(1)}, f32[2048,256]{1,0:T(8,128)}, u32[]{:S(2)}) copy-start(f32[2048,256]{1,0:T(8,128)} %cold_ref.1) | copy-start | bytes 6291460
  3.5 1.2 %copy-start.1 = (bf16[2048,256]{1,0:T(8,128)(2,1)S(1)}, bf16[2048,256]{1,0:T(8,128)(2,1)}, u32[]{:S(2)}) copy-start(bf16[2048,256]{1,0:T(8,128)(2,1)} %hot_ref.1) | copy-start | bytes 3145732
  4.7 0.9 %copy-start.2 = (bf16[256,256]{1,0:T(8,128)(2,1)S(1)}, bf16[256,256]{1,0:T(8,128)(2,1)}, u32[]{:S(2)}) copy-start(bf16[256,256]{1,0:T(8,128)(2,1)} %req_ref.1) | copy-start | bytes 393220
  5.6 0.7 copy-start.3
  6.3 0.7 copy-start.4
  7.0 0.7 copy-start.5
  7.7 0.7 copy-start.6
